TPU v7x, 32 devices: a whole 2x2x4 slice. The times are simulated.
32 devices in a mesh: grp: 2 (over y), pix: 4 (over z), frm: 2 (over x), sub: 2 (over core).
Axes of the slice: x: 2, y: 2, z: 4, core: 2. Of those that a mesh axis runs over, the one named last changes fastest.
Arguments:
- frames: bfloat16 [8192, 2, 4096], P(('grp', 'frm', 'sub'), None, 'pix'), parts along dimension 0, may hold values from -110 to 110
Outputs:
- covariance: float32 [8192, 1024], P(('grp', 'pix', 'frm', 'sub')), parts along dimension 0
There are 2 independent parts, one for each index of `grp`. A program takes and returns all parts, laid end to end along the dimension named above; each array names one. Nothing has to cross between parts.
All inputs are finite; a program needn't handle non-finite values.
Results may differ from a plain program's by a relative error of at most 0.0003.
Values may be sent and summed in bfloat16 or wider, within the bound.
A program may use at most 64 MiB of HBM per device.

v0:
```python
import jax
import jax.numpy as jnp
from jax import lax
from jax.sharding import PartitionSpec as P


def passed_along(value, axis, steps):
    count = lax.axis_size(axis)
    pairs = [(source, (source + steps) % count) for source in range(count)]
    return lax.ppermute(value, axis, pairs)


def pair_products(left, right):
    return jnp.einsum("fi,fj->ij", left, right, preferred_element_type=jnp.float32)


def shards(frames):
    frame_count = frames.shape[0] * lax.axis_size(("frm", "sub"))
    block = frames.shape[2]
    own_lower = frames[:, 0, :]
    own_upper = frames[:, 1, :]
    cycle = lax.axis_size("pix")
    offset = max(cycle // 4, 1)
    visitor = passed_along(own_upper, "pix", offset)
    sums_lower, sums_upper = lax.psum(
        (
            jnp.sum(own_lower, axis=0, dtype=jnp.float32),
            jnp.sum(visitor, axis=0, dtype=jnp.float32),
        ),
        ("frm", "sub"),
    )
    mean_lower = sums_lower / frame_count
    mean_upper = sums_upper / frame_count
    rows = block // lax.axis_size(("frm", "sub"))
    gram = lax.psum_scatter(
        pair_products(own_lower, visitor), ("frm", "sub"), scatter_dimension=0, tiled=True
    )
    first = lax.axis_index(("frm", "sub")) * rows
    chosen = lax.dynamic_slice_in_dim(mean_lower, first, rows, 0)
    return gram / frame_count - chosen[:, None] * mean_upper[None, :]


def solution(mesh):
    placed = (P(("grp", "frm", "sub"), None, "pix"),)
    return jax.shard_map(
        shards,
        mesh=mesh,
        in_specs=placed,
        out_specs=P(("grp", "pix", "frm", "sub"), None),
        check_vma=False,
    )
```

profile of v0, /device:TPU:0, one launch (start us, length us, event | category | flops | bytes accessed | tf_op | source)
XLA Modules:
  0.0 125.1 jit_solution(12777637941520766462)
XLA Ops:
  6.5 0.0 reduce-scatter.2.cloned.1.call-start
  6.5 9.1 %fusion.1 = (bf16[1024,1,1024]{2,1,0:T(2,128)(2,1)S(1)}, bf16[1024,1,1024]{2,1,0:T(2,128)(2,1)S(1)}) fusion(bf16[1024,2,1024]{2,1,0:T(2,128)(2,1)} %param.1), kind=kLoop, calls=%fused_computation.8 | loop fusion | bytes 8388608 | tf_op jit(solution)/shard_map/slice | solution.py:20
  15.7 0.0 copy-start
  15.7 0.8 copy.11
  16.5 3.1 %collective-permute-start = (bf16[1024,1024]{1,0:T(8,128)(2,1)S(1)}, bf16[1024,1024]{1,0:T(8,128)(2,1)S(1)}, u32[]{:S(2)}, u32[]{:S(2)}) collective-permute-start(bf16[1024,1024]{1,0:T(8,128)(2,1)S(1)} %bitcast.9), channel_id=1, source_target_pairs={{0,4},{4,8},{8,12},{12,0},{1,5},{5,9},{9,13},{13,1},{2,6},{6,10},{... | collective-permute-start | bytes 6291464 | tf_op jit(solution)/shard_map/ppermute | solution.py:10
  19.6 47.7 %collective-permute-done = bf16[1024,1024]{1,0:T(8,128)(2,1)S(1)} collective-permute-done((bf16[1024,1024]{1,0:T(8,128)(2,1)S(1)}, bf16[1024,1024]{1,0:T(8,128)(2,1)S(1)}, u32[]{:S(2)}, u32[]{:S(2)}) %collective-permute-start) | collective-permute-done | bytes 2097184 | tf_op jit(solution)/shard_map/ppermute | solution.py:10
  67.3 0.0 copy-done
  67.3 4.6 %fusion = f32[1024,1024]{1,0:T(8,128)} fusion(bf16[1024,1024]{1,0:T(8,128)(2,1)S(1)} %collective-permute-done, bf16[1024,1,1024]{2,1,0:T(2,128)(2,1)S(1)} %get-tuple-element.7), kind=kOutput, calls=%fused_computation.5 | convolution fusion | flops 2147483648 | bytes 8388608 | tf_op jit(solution)/shard_map/fi,fj->ij/dot_general | solution.py:14
  71.9 0.0 reduce-scatter.2.cloned.1.call-update
  71.9 2.8 %convert_reduce_fusion.1 = f32[1024]{0:T(1024)S(1)} fusion(bf16[1024,1,1024]{2,1,0:T(2,128)(2,1)} %copy-done), kind=kLoop, calls=%fused_computation.1 | loop fusion | flops 2096128 | bytes 2101248 | tf_op jit(solution)/shard_map/reduce_sum | solution.py:27
  74.7 0.4 convert_reduce_fusion
  75.0 5.9 %all-reduce = (f32[1024]{0:T(1024)S(1)}, f32[1024]{0:T(1024)S(1)}) all-reduce(f32[1024]{0:T(1024)S(1)} %convert_reduce_fusion, f32[1024]{0:T(1024)S(1)} %convert_reduce_fusion.1), channel_id=1, replica_groups=mesh['grp'=2,'pix'=4,'frm'=2,'sub'=2] {'frm','sub'}, use_global_device_ids=true, to_apply=%region_4.0 | all-reduce | flops 2048 | bytes 16384 | tf_op jit(solution)/shard_map/psum | solution.py:25
  80.9 0.1 dynamic_slice.3
  81.0 34.9 %reduce-scatter.2.cloned.1.call-done = f32[256,1024]{1,0:T(8,128)} async-done(((f32[1024,1024]{1,0:T(8,128)}), f32[256,1024]{1,0:T(8,128)}) %reduce-scatter.2.cloned.1.call-update) | async-done | bytes 1048592 | tf_op jit(solution)/shard_map/reduce_scatter | solution.py:35
  115.9 2.4 %multiply_subtract_fusion = f32[256,1024]{1,0:T(8,128)} fusion(f32[256,1024]{1,0:T(8,128)} %reduce-scatter.2.cloned.1.call-done, f32[1024]{0:T(1024)S(1)} %get-tuple-element.9, f32[256]{0:T(256)S(1)} %dynamic_slice.3), kind=kLoop, calls=%fused_computation.4 | loop fusion | flops 786432 | bytes 2102272 | tf_op jit(solution)/shard_map/sub | solution.py:40
  (1 shorter events, 0.0 us)
Async XLA Ops:
  6.5 109.4 %reduce-scatter.2.cloned.1.call-start = ((), (), s32[]{:S(2)}) async-start(), calls=%async_computation.1 | async-start | bytes 5242880 | tf_op jit(solution)/shard_map/reduce_scatter | solution.py:35
  15.7 51.6 %copy-start = (bf16[1024,1,1024]{2,1,0:T(2,128)(2,1)}, bf16[1024,1,1024]{2,1,0:T(2,128)(2,1)S(1)}, u32[]{:S(2)}) copy-start(bf16[1024,1,1024]{2,1,0:T(2,128)(2,1)S(1)} %get-tuple-element.7) | copy-start | bytes 6291460
  16.5 50.7 %collective-permute-start = (bf16[1024,1024]{1,0:T(8,128)(2,1)S(1)}, bf16[1024,1024]{1,0:T(8,128)(2,1)S(1)}, u32[]{:S(2)}, u32[]{:S(2)}) collective-permute-start(bf16[1024,1024]{1,0:T(8,128)(2,1)S(1)} %bitcast.9), channel_id=1, source_target_pairs={{0,4},{4,8},{8,12},{12,0},{1,5},{5,9},{9,13},{13,1},{2,6},{6,10},{... | collective-permute-start | bytes 6291464 | tf_op jit(solution)/shard_map/ppermute | solution.py:10
Sparse Core Ops, SparseCore 0:
  72.0 43.8 reduce-scatter.1
where the time goes:
time: 125 us
  waiting for transfers between devices  82.6 us (66%)
  between operations  13.4 us (11%)
  local copies, waits for them, and re-layouts  10.1 us (8%)
  blocking collectives  5.89 us (5%)
  other arithmetic  5.51 us (4%)
  matrix products  4.59 us (4%)
  starting transfers between devices  3.08 us (2%)
    ppermute x1, waiting for transfers between devices, passed_along(): return lax.ppermute(value, axis, pairs)  47.7 us
    reduce_scatter x1, waiting for transfers between devices, shards(): lax.psum_scatter(pair_products(own_lower, visitor), ('frm', 'sub'), scatt...  34.9 us
    slice x1, local copies, waits for them, and re-layouts, shards(): own_lower = frames[:, 0, :]  9.13 us
    psum x1, blocking collectives, shards(): lax.psum((jnp.sum(own_lower, axis=0, dtype=jnp.float32), jnp.sum(visitor,...  5.89 us
    dot_general x1, matrix products, pair_products(): jnp.einsum('fi,fj->ij', left, right, preferred_element_type=jnp.float32)  4.59 us
    ppermute x1, starting transfers between devices, passed_along(): return lax.ppermute(value, axis, pairs)  3.08 us
    reduce_sum x1, other arithmetic, shards(): jnp.sum(own_lower, axis=0, dtype=jnp.float32)  2.78 us
  transfers between devices with their start and end apart: 2, of which 2 were waited for; matrix products, arithmetic and copies ran while one was open for 3% of the time, Pallas kernels for 0%

commit v1 on v0

v1 whole, which is shorter than its diff:
```python
import functools

import jax
import jax.numpy as jnp
from jax import lax
from jax.experimental import pallas as pl
from jax.experimental.pallas import tpu as pltpu
from jax.sharding import PartitionSpec as P

MESH = pl.DeviceIdType.MESH
WIDTH = 128
GROUP = 128
SUMS = 8


def selector(half):
    row = lax.broadcasted_iota(jnp.int32, (GROUP, 2 * GROUP), 0)
    column = lax.broadcasted_iota(jnp.int32, (GROUP, 2 * GROUP), 1)
    return jnp.where(column == 2 * row + half, 1.0, 0.0).astype(jnp.bfloat16)


def product(left, right):
    return jnp.dot(left, right, preferred_element_type=jnp.float32)


def kernel(
    n_pix, n_frm, offset,
    frames_ref, out_ref,
    mixed, upper, visitor, twin, lower, lower_twin, own, outgoing, incoming,
    sums_out, sums_in, mean_lower,
    load_sem, z_send, z_recv, f_send, f_recv, x_send, x_recv, l_send, l_recv, s_send, s_recv,
):
    frame_count, _, block = frames_ref.shape
    chunks = block // WIDTH
    rows = out_ref.shape[0]
    total = frame_count * n_frm * 2
    pix, frm, sub = lax.axis_index("pix"), lax.axis_index("frm"), lax.axis_index("sub")
    ahead = {"pix": lax.rem(pix + offset, n_pix)}
    behind = {"pix": lax.rem(pix + n_pix - offset, n_pix)}
    sibling = {"sub": 1 - sub}
    peers = [lax.rem(frm + 1 + k, n_frm) for k in range(n_frm - 1)]

    def load(c):
        columns = pl.ds(c * WIDTH, WIDTH)
        return pltpu.make_async_copy(frames_ref.at[:, :, columns], mixed.at[c], load_sem.at[c])

    def remote(src, dst, send, recv, device):
        return pltpu.make_async_remote_copy(
            src_ref=src, dst_ref=dst, send_sem=send, recv_sem=recv, device_id=device, device_id_type=MESH
        )

    def pass_on(c):
        return remote(upper.at[c], visitor.at[c], z_send.at[c], z_recv.at[c], ahead)

    def share(c):
        return remote(visitor.at[c], twin.at[c], f_send.at[c], f_recv.at[c], sibling)

    def give(c, k):
        return remote(
            outgoing.at[c, k], incoming.at[c, k], x_send.at[c, k], x_recv.at[c, k], {"frm": peers[k]}
        )

    def rows_of(f, s):
        return pl.ds(pl.multiple_of((f * 2 + s) * rows, rows), rows)

    def share_lower(f):
        return remote(lower.at[rows_of(f, 1 - sub)], lower_twin.at[f], l_send.at[f], l_recv.at[f], sibling)

    def give_sums(k):
        return remote(sums_out.at[k], sums_in.at[k], s_send.at[k], s_recv.at[k], {"frm": peers[k]})

    load(0).start()
    load(1).start()
    barrier = pltpu.get_barrier_semaphore()
    neighbours = [ahead, behind, sibling] + [{"frm": f} for f in peers]
    for device in neighbours:
        pl.semaphore_signal(barrier, inc=1, device_id=device, device_id_type=MESH)

    pick_upper, pick_lower = selector(1), selector(0)
    for c in range(chunks):
        load(c).wait()
        if c + 2 < chunks:
            load(c + 2).start()
        for g in range(frame_count // GROUP):
            part = mixed[c, pl.ds(g * GROUP, GROUP)].reshape(2 * GROUP, WIDTH)
            upper[c, pl.ds(g * GROUP, GROUP)] = product(pick_upper, part).astype(jnp.bfloat16)
        if c == 0:
            pl.semaphore_wait(barrier, len(neighbours))
        pass_on(c).start()

    def separate(c, _):
        for g in range(frame_count // GROUP):
            part = mixed[c, pl.ds(g * GROUP, GROUP)].reshape(2 * GROUP, WIDTH)
            lower[pl.ds(pl.multiple_of(c * WIDTH, WIDTH), WIDTH), pl.ds(g * GROUP, GROUP)] = (
                product(pick_lower, part).T.astype(jnp.bfloat16)
            )
        return 0

    lax.fori_loop(0, chunks, separate, 0)
    for f in range(n_frm):
        share_lower(f).start()
    for f in range(n_frm):
        share_lower(f).wait_recv()
    ones = jnp.ones((frame_count, 128), jnp.bfloat16)
    for k in range(n_frm - 1):
        sums_out[k] = product(lower[rows_of(peers[k], sub)], ones) + product(lower_twin[peers[k]], ones)
        give_sums(k).start()
    own_sums = product(lower[rows_of(frm, sub)], ones) + product(lower_twin[frm], ones)
    for k in range(n_frm - 1):
        give_sums(k).wait_recv()
        own_sums += sums_in[k]
    mean_lower[...] = own_sums / total

    ones_row = jnp.ones((16, frame_count), jnp.bfloat16)

    def finish(c):
        gram = own[c]
        for k in range(n_frm - 1):
            give(c, k).wait_recv()
            gram += incoming[c, k]
        mean_upper = gram[rows : rows + 1] / total
        out_ref[:, pl.ds(pl.multiple_of(c * WIDTH, WIDTH), WIDTH)] = (
            gram[:rows] / total - mean_lower[...] * mean_upper
        )

    def step(c, _):
        pass_on(c).wait_recv()
        share(c).start()

        def pair(f):
            return product(lower[rows_of(f, sub)], visitor[c]) + product(lower_twin[f], twin[c])

        share(c).wait_recv()
        column_sums = (product(ones_row, visitor[c]) + product(ones_row, twin[c]))[:SUMS]
        for k in range(n_frm - 1):
            outgoing[c, k, :rows] = pair(peers[k])
            outgoing[c, k, rows:] = column_sums
            give(c, k).start()
        own[c, :rows] = pair(frm)
        own[c, rows:] = column_sums

        @pl.when(c > 0)
        def _():
            finish(c - 1)

        return 0

    lax.fori_loop(0, chunks, step, 0)
    finish(chunks - 1)

    for f in range(n_frm):
        share_lower(f).wait_send()
    for k in range(n_frm - 1):
        give_sums(k).wait_send()

    def drain(c, _):
        pass_on(c).wait_send()
        share(c).wait_send()
        for k in range(n_frm - 1):
            give(c, k).wait_send()
        return 0

    lax.fori_loop(0, chunks, drain, 0)


def shards(n_pix, n_frm, n_sub, frames):
    frame_count, _, block = frames.shape
    assert n_sub == 2
    chunks, rows, others = block // WIDTH, block // (n_frm * 2), n_frm - 1
    f32, bf16 = jnp.float32, jnp.bfloat16
    dma = pltpu.SemaphoreType.DMA
    return pl.pallas_call(
        functools.partial(kernel, n_pix, n_frm, max(n_pix // 4, 1)),
        out_shape=jax.ShapeDtypeStruct((rows, block), f32),
        in_specs=[pl.BlockSpec(memory_space=pl.ANY)],
        out_specs=pl.BlockSpec(memory_space=pltpu.VMEM),
        scratch_shapes=[
            pltpu.VMEM((chunks, frame_count, 2, WIDTH), bf16),
            pltpu.VMEM((chunks, frame_count, WIDTH), bf16),
            pltpu.VMEM((chunks, frame_count, WIDTH), bf16),
            pltpu.VMEM((chunks, frame_count, WIDTH), bf16),
            pltpu.VMEM((block, frame_count), bf16),
            pltpu.VMEM((n_frm, rows, frame_count), bf16),
            pltpu.VMEM((chunks, rows + SUMS, WIDTH), f32),
            pltpu.VMEM((chunks, others, rows + SUMS, WIDTH), f32),
            pltpu.VMEM((chunks, others, rows + SUMS, WIDTH), f32),
            pltpu.VMEM((others, rows, 128), f32),
            pltpu.VMEM((others, rows, 128), f32),
            pltpu.VMEM((rows, 128), f32),
            dma((chunks,)), dma((chunks,)), dma((chunks,)), dma((chunks,)), dma((chunks,)),
            dma((chunks, others)), dma((chunks, others)),
            dma((n_frm,)), dma((n_frm,)), dma((others,)), dma((others,)),
        ],
        compiler_params=pltpu.CompilerParams(
            collective_id=0, has_side_effects=True, vmem_limit_bytes=60 << 20
        ),
        cost_estimate=pl.CostEstimate(
            flops=2 * frame_count * block * block, bytes_accessed=4 * frame_count * block, transcendentals=0
        ),
    )(frames)


def solution(mesh):
    shape = mesh.shape
    return jax.shard_map(
        functools.partial(shards, shape["pix"], shape["frm"], shape["sub"]),
        mesh=mesh,
        in_specs=(P(("grp", "frm", "sub"), None, "pix"),),
        out_specs=P(("grp", "pix", "frm", "sub"), None),
        check_vma=False,
    )
```

time: 125 us -> 62.6 us (0.50)
  waiting for transfers between devices: 82.6 us -> 0 us
  Pallas kernels: 0 us -> 60.1 us
  between operations: 13.4 us -> 0.01 us
  local copies, waits for them, and re-layouts: 10.1 us -> 2.31 us
  blocking collectives: 5.89 us -> 0 us
  other arithmetic: 5.51 us -> 0 us
  matrix products: 4.59 us -> 0 us
  starting transfers between devices: 3.08 us -> 0 us
    pallas_call x0 -> x1, Pallas kernels: none -> 60.1 us  [shards(): pl.pallas_call(functools.partial(kernel, n_pix, n_frm, max(n_pix // 4, 1)...]
    ppermute x1 -> x0, waiting for transfers between devices: 47.7 us -> none  [passed_along(): return lax.ppermute(value, axis, pairs)]
    reduce_scatter x1 -> x0, waiting for transfers between devices: 34.9 us -> none  [shards(): lax.psum_scatter(pair_products(own_lower, visitor), ('frm', 'sub'), scatt...]
    slice x1 -> x0, local copies, waits for them, and re-layouts: 9.13 us -> none  [shards(): own_lower = frames[:, 0, :]]
    psum x1 -> x0, blocking collectives: 5.89 us -> none  [shards(): lax.psum((jnp.sum(own_lower, axis=0, dtype=jnp.float32), jnp.sum(visitor,...]
    dot_general x1 -> x0, matrix products: 4.59 us -> none  [pair_products(): jnp.einsum('fi,fj->ij', left, right, preferred_element_type=jnp.float32)]
    reduce_sum x2 -> x0, other arithmetic: 3.15 us -> none  [the longest x1 2.78 us: shards(): jnp.sum(own_lower, axis=0, dtype=jnp.float32)]
    ppermute x1 -> x0, starting transfers between devices: 3.08 us -> none  [passed_along(): return lax.ppermute(value, axis, pairs)]
  transfers between devices with their start and end apart: 2 -> 0, of which waited for: 2 -> 0; matrix products, arithmetic and copies ran while one was open for 3% -> 0% of each run, Pallas kernels for 0% -> 0%
where the time goes in v1:
time: 62.6 us; the launch traced here: 62.4 us
  Pallas kernels  60.1 us (96%)
  local copies, waits for them, and re-layouts  2.31 us (4%)
    pallas_call x1, Pallas kernels, shards(): pl.pallas_call(functools.partial(kernel, n_pix, n_frm, max(n_pix // 4, 1)...  60.1 us
    unnamed x1, local copies, waits for them, and re-layouts  2.31 us

profile of v1, /device:TPU:0, one launch (start us, length us, event | category | flops | bytes accessed | tf_op | source)
XLA Modules:
  0.0 62.4 jit_solution(1041070280233858934)
XLA Ops:
  0.0 60.1 %shard_map.17 = f32[256,1024]{1,0:T(8,128)} custom-call(bf16[1024,2,1024]{2,1,0:T(2,128)(2,1)} %frames_ref.1), custom_call_target="tpu_custom_call" | custom-call | flops 2147483648 | bytes 4194304 | tf_op jit(solution)/shard_map/pallas_call | solution.py:172
  60.1 2.3 %copy.3 = f32[256,1024]{1,0:T(8,128)} copy(f32[256,1024]{1,0:T(8,128)} %shard_map.17) | data formatting | bytes 2097152

commit v2 on v1

--- a/solution.py
+++ b/solution.py
@@ -10,6 +10,7 @@
 MESH = pl.DeviceIdType.MESH
 WIDTH = 128
 GROUP = 128
+PIECES = 4
 SUMS = 8
 
 
@@ -28,7 +29,7 @@
     frames_ref, out_ref,
     mixed, upper, visitor, twin, lower, lower_twin, own, outgoing, incoming,
     sums_out, sums_in, mean_lower,
-    load_sem, z_send, z_recv, f_send, f_recv, x_send, x_recv, l_send, l_recv, s_send, s_recv,
+    load_sem, piece_load, piece_send, piece_recv, z_send, z_recv, f_send, f_recv, x_send, x_recv, l_send, l_recv, s_send, s_recv,
 ):
     frame_count, _, block = frames_ref.shape
     chunks = block // WIDTH
@@ -40,9 +41,15 @@
     sibling = {"sub": 1 - sub}
     peers = [lax.rem(frm + 1 + k, n_frm) for k in range(n_frm - 1)]
 
+    piece = frame_count // PIECES
+
     def load(c):
         columns = pl.ds(c * WIDTH, WIDTH)
         return pltpu.make_async_copy(frames_ref.at[:, :, columns], mixed.at[c], load_sem.at[c])
+
+    def load_piece(i):
+        run = pl.ds(i * piece, piece)
+        return pltpu.make_async_copy(frames_ref.at[run, :, pl.ds(0, WIDTH)], mixed.at[0, run], piece_load.at[i])
 
     def remote(src, dst, send, recv, device):
         return pltpu.make_async_remote_copy(
@@ -52,6 +59,10 @@
     def pass_on(c):
         return remote(upper.at[c], visitor.at[c], z_send.at[c], z_recv.at[c], ahead)
 
+    def pass_on_piece(i):
+        run = pl.ds(i * piece, piece)
+        return remote(upper.at[0, run], visitor.at[0, run], piece_send.at[i], piece_recv.at[i], ahead)
+
     def share(c):
         return remote(visitor.at[c], twin.at[c], f_send.at[c], f_recv.at[c], sibling)
 
@@ -69,7 +80,8 @@
     def give_sums(k):
         return remote(sums_out.at[k], sums_in.at[k], s_send.at[k], s_recv.at[k], {"frm": peers[k]})
 
-    load(0).start()
+    for i in range(PIECES):
+        load_piece(i).start()
     load(1).start()
     barrier = pltpu.get_barrier_semaphore()
     neighbours = [ahead, behind, sibling] + [{"frm": f} for f in peers]
@@ -77,15 +89,24 @@
         pl.semaphore_signal(barrier, inc=1, device_id=device, device_id_type=MESH)
 
     pick_upper, pick_lower = selector(1), selector(0)
-    for c in range(chunks):
+
+    def separate_upper(c, first, last):
+        for g in range(first // GROUP, last // GROUP):
+            part = mixed[c, pl.ds(g * GROUP, GROUP)].reshape(2 * GROUP, WIDTH)
+            upper[c, pl.ds(g * GROUP, GROUP)] = product(pick_upper, part).astype(jnp.bfloat16)
+
+    for i in range(PIECES):
+        load_piece(i).wait()
+        separate_upper(0, i * piece, (i + 1) * piece)
+        if i == 0:
+            pl.semaphore_wait(barrier, len(neighbours))
+        pass_on_piece(i).start()
+    load(2).start()
+    for c in range(1, chunks):
         load(c).wait()
         if c + 2 < chunks:
             load(c + 2).start()
-        for g in range(frame_count // GROUP):
-            part = mixed[c, pl.ds(g * GROUP, GROUP)].reshape(2 * GROUP, WIDTH)
-            upper[c, pl.ds(g * GROUP, GROUP)] = product(pick_upper, part).astype(jnp.bfloat16)
-        if c == 0:
-            pl.semaphore_wait(barrier, len(neighbours))
+        separate_upper(c, 0, frame_count)
         pass_on(c).start()
 
     def separate(c, _):
@@ -124,7 +145,15 @@
         )
 
     def step(c, _):
-        pass_on(c).wait_recv()
+        @pl.when(c == 0)
+        def _():
+            for i in range(PIECES):
+                pass_on_piece(i).wait_recv()
+
+        @pl.when(c > 0)
+        def _():
+            pass_on(c).wait_recv()
+
         share(c).start()
 
         def pair(f):
@@ -154,7 +183,15 @@
         give_sums(k).wait_send()
 
     def drain(c, _):
-        pass_on(c).wait_send()
+        @pl.when(c == 0)
+        def _():
+            for i in range(PIECES):
+                pass_on_piece(i).wait_send()
+
+        @pl.when(c > 0)
+        def _():
+            pass_on(c).wait_send()
+
         share(c).wait_send()
         for k in range(n_frm - 1):
             give(c, k).wait_send()
@@ -165,7 +202,7 @@
 
 def shards(n_pix, n_frm, n_sub, frames):
     frame_count, _, block = frames.shape
-    assert n_sub == 2
+    assert n_sub == 2 and block > 2 * WIDTH
     chunks, rows, others = block // WIDTH, block // (n_frm * 2), n_frm - 1
     f32, bf16 = jnp.float32, jnp.bfloat16
     dma = pltpu.SemaphoreType.DMA
@@ -187,12 +224,13 @@
             pltpu.VMEM((others, rows, 128), f32),
             pltpu.VMEM((others, rows, 128), f32),
             pltpu.VMEM((rows, 128), f32),
-            dma((chunks,)), dma((chunks,)), dma((chunks,)), dma((chunks,)), dma((chunks,)),
+            dma((chunks,)), dma((PIECES,)), dma((PIECES,)), dma((PIECES,)),
+            dma((chunks,)), dma((chunks,)), dma((chunks,)), dma((chunks,)),
             dma((chunks, others)), dma((chunks, others)),
             dma((n_frm,)), dma((n_frm,)), dma((others,)), dma((others,)),
         ],
         compiler_params=pltpu.CompilerParams(
-            collective_id=0, has_side_effects=True, vmem_limit_bytes=60 << 20
+            collective_id=0, has_side_effects=True, vmem_limit_bytes=51 << 20
         ),
         cost_estimate=pl.CostEstimate(
             flops=2 * frame_count * block * block, bytes_accessed=4 * frame_count * block, transcendentals=0

time: 62.6 us -> 60 us (0.958)
  local copies, waits for them, and re-layouts: 2.31 us -> 0.97 us
  Pallas kernels: 60.1 us -> 58.8 us
    unnamed x1, local copies, waits for them, and re-layouts: 2.31 us -> 0.97 us
    pallas_call x1, Pallas kernels: 60.1 us -> 58.8 us  [shards(): pl.pallas_call(functools.partial(kernel, n_pix, n_frm, max(n_pix // 4, 1)...]
where the time goes in v2:
time: 60 us; the launch traced here: 59.8 us
  Pallas kernels  58.8 us (98%)
  local copies, waits for them, and re-layouts  0.97 us (2%)
    pallas_call x1, Pallas kernels, shards(): pl.pallas_call(functools.partial(kernel, n_pix, n_frm, max(n_pix // 4, 1)...  58.8 us

profile of v2, /device:TPU:0, one launch (start us, length us, event | category | flops | bytes accessed | tf_op | source)
XLA Modules:
  0.0 59.8 jit_solution(215644202618125131)
XLA Ops:
  0.0 58.8 %shard_map.17 = f32[256,1024]{1,0:T(8,128)S(1)} custom-call(bf16[1024,2,1024]{2,1,0:T(2,128)(2,1)} %frames_ref.1), custom_call_target="tpu_custom_call" | custom-call | flops 2147483648 | bytes 4194304 | tf_op jit(solution)/shard_map/pallas_call | solution.py:209
  58.8 1.0 %copy.3 = f32[256,1024]{1,0:T(8,128)} copy(f32[256,1024]{1,0:T(8,128)S(1)} %shard_map.17) | data formatting | bytes 2097152

commit v3 on v2

--- a/solution.py
+++ b/solution.py
@@ -24,12 +24,23 @@
     return jnp.dot(left, right, preferred_element_type=jnp.float32)
 
 
+def swapped(value):
+    return pltpu.roll(value, WIDTH // 2, 1)
+
+
+def joined(left, right):
+    lane = lax.broadcasted_iota(jnp.int32, left.shape, 1)
+    return jnp.where(lane < WIDTH // 2, left, right)
+
+
 def kernel(
     n_pix, n_frm, offset,
     frames_ref, out_ref,
     mixed, upper, visitor, twin, lower, lower_twin, own, outgoing, incoming,
     sums_out, sums_in, mean_lower,
+    upper_half, visitor_half, twin_half, own_half, outgoing_half, incoming_half,
     load_sem, piece_load, piece_send, piece_recv, z_send, z_recv, f_send, f_recv, x_send, x_recv, l_send, l_recv, s_send, s_recv,
+    hz_send, hz_recv, hf_send, hf_recv, hx_send, hx_recv,
 ):
     frame_count, _, block = frames_ref.shape
     chunks = block // WIDTH
@@ -71,6 +82,17 @@
             outgoing.at[c, k], incoming.at[c, k], x_send.at[c, k], x_recv.at[c, k], {"frm": peers[k]}
         )
 
+    def pass_on_half(h):
+        return remote(upper_half.at[h], visitor_half.at[h], hz_send.at[h], hz_recv.at[h], ahead)
+
+    def share_half(h):
+        return remote(visitor_half.at[h], twin_half.at[h], hf_send.at[h], hf_recv.at[h], sibling)
+
+    def give_half(h, k):
+        return remote(
+            outgoing_half.at[h, k], incoming_half.at[h, k], hx_send.at[h, k], hx_recv.at[h, k], {"frm": peers[k]}
+        )
+
     def rows_of(f, s):
         return pl.ds(pl.multiple_of((f * 2 + s) * rows, rows), rows)
 
@@ -102,12 +124,23 @@
             pl.semaphore_wait(barrier, len(neighbours))
         pass_on_piece(i).start()
     load(2).start()
-    for c in range(1, chunks):
+    for c in range(1, chunks - 1):
         load(c).wait()
         if c + 2 < chunks:
             load(c + 2).start()
         separate_upper(c, 0, frame_count)
         pass_on(c).start()
+    last, middle, half_rows = chunks - 1, frame_count // 2, rows // 2
+    load(last).wait()
+    for g in range(middle // GROUP):
+        early, late = (
+            product(pick_upper, mixed[last, pl.ds(first, GROUP)].reshape(2 * GROUP, WIDTH))
+            for first in (g * GROUP, middle + g * GROUP)
+        )
+        upper_half[0, pl.ds(g * GROUP, GROUP)] = joined(early, swapped(late)).astype(jnp.bfloat16)
+        upper_half[1, pl.ds(g * GROUP, GROUP)] = joined(swapped(early), late).astype(jnp.bfloat16)
+    for h in range(2):
+        pass_on_half(h).start()
 
     def separate(c, _):
         for g in range(frame_count // GROUP):
@@ -174,8 +207,52 @@
 
         return 0
 
-    lax.fori_loop(0, chunks, step, 0)
-    finish(chunks - 1)
+    lax.fori_loop(0, last, step, 0)
+
+    def step_half(h):
+        pass_on_half(h).wait_recv()
+        share_half(h).start()
+
+        def pair(f):
+            def over(run):
+                return product(lower[rows_of(f, sub), run], visitor_half[h]) + product(
+                    lower_twin[f, :, run], twin_half[h]
+                )
+
+            early, late = over(slice(0, middle)), over(slice(middle, frame_count))
+            return joined(
+                early[:half_rows] + swapped(late[:half_rows]), swapped(early[half_rows:]) + late[half_rows:]
+            )
+
+        share_half(h).wait_recv()
+        column_sums = (
+            product(ones_row[:, :middle], visitor_half[h]) + product(ones_row[:, :middle], twin_half[h])
+        )[:SUMS]
+        column_sums = column_sums + swapped(column_sums)
+        for k in range(n_frm - 1):
+            outgoing_half[h, k, :half_rows] = pair(peers[k])
+            outgoing_half[h, k, half_rows:] = column_sums
+            give_half(h, k).start()
+        own_half[h, :half_rows] = pair(frm)
+        own_half[h, half_rows:] = column_sums
+
+    def finished_half(h):
+        gram = own_half[h]
+        for k in range(n_frm - 1):
+            give_half(h, k).wait_recv()
+            gram += incoming_half[h, k]
+        mean_upper = gram[half_rows : half_rows + 1] / total
+        means = joined(mean_lower[:half_rows], mean_lower[half_rows:])
+        return gram[:half_rows] / total - means * mean_upper
+
+    step_half(0)
+    finish(last - 1)
+    step_half(1)
+    first_half = finished_half(0)
+    second_half = finished_half(1)
+    columns = pl.ds(last * WIDTH, WIDTH)
+    out_ref[:half_rows, columns] = joined(first_half, swapped(second_half))
+    out_ref[half_rows:, columns] = joined(swapped(first_half), second_half)
 
     for f in range(n_frm):
         share_lower(f).wait_send()
@@ -197,7 +274,12 @@
             give(c, k).wait_send()
         return 0
 
-    lax.fori_loop(0, chunks, drain, 0)
+    lax.fori_loop(0, last, drain, 0)
+    for h in range(2):
+        pass_on_half(h).wait_send()
+        share_half(h).wait_send()
+        for k in range(n_frm - 1):
+            give_half(h, k).wait_send()
 
 
 def shards(n_pix, n_frm, n_sub, frames):
@@ -224,10 +306,17 @@
             pltpu.VMEM((others, rows, 128), f32),
             pltpu.VMEM((others, rows, 128), f32),
             pltpu.VMEM((rows, 128), f32),
+            pltpu.VMEM((2, frame_count // 2, WIDTH), bf16),
+            pltpu.VMEM((2, frame_count // 2, WIDTH), bf16),
+            pltpu.VMEM((2, frame_count // 2, WIDTH), bf16),
+            pltpu.VMEM((2, rows // 2 + SUMS, WIDTH), f32),
+            pltpu.VMEM((2, others, rows // 2 + SUMS, WIDTH), f32),
+            pltpu.VMEM((2, others, rows // 2 + SUMS, WIDTH), f32),
             dma((chunks,)), dma((PIECES,)), dma((PIECES,)), dma((PIECES,)),
             dma((chunks,)), dma((chunks,)), dma((chunks,)), dma((chunks,)),
             dma((chunks, others)), dma((chunks, others)),
             dma((n_frm,)), dma((n_frm,)), dma((others,)), dma((others,)),
+            dma((2,)), dma((2,)), dma((2,)), dma((2,)), dma((2, others)), dma((2, others)),
         ],
         compiler_params=pltpu.CompilerParams(
             collective_id=0, has_side_effects=True, vmem_limit_bytes=51 << 20

time: 60 us -> 60 us (level)
  no operation moved by 1% of the time
where the time goes in v3:
time: 60 us; the launch traced here: 59.8 us
  Pallas kernels  58.8 us (98%)
  local copies, waits for them, and re-layouts  0.97 us (2%)
    pallas_call x1, Pallas kernels, shards(): pl.pallas_call(functools.partial(kernel, n_pix, n_frm, max(n_pix // 4, 1)...  58.8 us

profile of v3, /device:TPU:0, one launch (start us, length us, event | category | flops | bytes accessed | tf_op | source)
XLA Modules:
  0.0 59.8 jit_solution(9293742092592187321)
XLA Ops:
  0.0 58.8 %shard_map.17 = f32[256,1024]{1,0:T(8,128)S(1)} custom-call(bf16[1024,2,1024]{2,1,0:T(2,128)(2,1)} %frames_ref.1), custom_call_target="tpu_custom_call" | custom-call | flops 2147483648 | bytes 4194304 | tf_op jit(solution)/shard_map/pallas_call | solution.py:291
  58.8 1.0 %copy.3 = f32[256,1024]{1,0:T(8,128)} copy(f32[256,1024]{1,0:T(8,128)S(1)} %shard_map.17) | data formatting | bytes 2097152

commit v4 on v3

--- a/solution.py
+++ b/solution.py
@@ -189,16 +189,16 @@
 
         share(c).start()
 
-        def pair(f):
-            return product(lower[rows_of(f, sub)], visitor[c]) + product(lower_twin[f], twin[c])
-
+        for k in range(n_frm - 1):
+            outgoing[c, k, :rows] = product(lower[rows_of(peers[k], sub)], visitor[c])
+        own[c, :rows] = product(lower[rows_of(frm, sub)], visitor[c])
         share(c).wait_recv()
         column_sums = (product(ones_row, visitor[c]) + product(ones_row, twin[c]))[:SUMS]
         for k in range(n_frm - 1):
-            outgoing[c, k, :rows] = pair(peers[k])
+            outgoing[c, k, :rows] += product(lower_twin[peers[k]], twin[c])
             outgoing[c, k, rows:] = column_sums
             give(c, k).start()
-        own[c, :rows] = pair(frm)
+        own[c, :rows] += product(lower_twin[frm], twin[c])
         own[c, rows:] = column_sums
 
         @pl.when(c > 0)
@@ -213,27 +213,25 @@
         pass_on_half(h).wait_recv()
         share_half(h).start()
 
-        def pair(f):
-            def over(run):
-                return product(lower[rows_of(f, sub), run], visitor_half[h]) + product(
-                    lower_twin[f, :, run], twin_half[h]
-                )
-
-            early, late = over(slice(0, middle)), over(slice(middle, frame_count))
+        def folded(left, right):
+            early, late = product(left[:, :middle], right), product(left[:, middle:], right)
             return joined(
                 early[:half_rows] + swapped(late[:half_rows]), swapped(early[half_rows:]) + late[half_rows:]
             )
 
+        for k in range(n_frm - 1):
+            outgoing_half[h, k, :half_rows] = folded(lower[rows_of(peers[k], sub)], visitor_half[h])
+        own_half[h, :half_rows] = folded(lower[rows_of(frm, sub)], visitor_half[h])
         share_half(h).wait_recv()
         column_sums = (
             product(ones_row[:, :middle], visitor_half[h]) + product(ones_row[:, :middle], twin_half[h])
         )[:SUMS]
         column_sums = column_sums + swapped(column_sums)
         for k in range(n_frm - 1):
-            outgoing_half[h, k, :half_rows] = pair(peers[k])
+            outgoing_half[h, k, :half_rows] += folded(lower_twin[peers[k]], twin_half[h])
             outgoing_half[h, k, half_rows:] = column_sums
             give_half(h, k).start()
-        own_half[h, :half_rows] = pair(frm)
+        own_half[h, :half_rows] += folded(lower_twin[frm], twin_half[h])
         own_half[h, half_rows:] = column_sums
 
     def finished_half(h):

time: 60 us -> 60.5 us (level)
  no operation moved by 1% of the time
where the time goes in v4:
time: 60.5 us; the launch traced here: 60.3 us
  Pallas kernels  59.4 us (98%)
  local copies, waits for them, and re-layouts  0.97 us (2%)
    pallas_call x1, Pallas kernels, shards(): pl.pallas_call(functools.partial(kernel, n_pix, n_frm, max(n_pix // 4, 1)...  59.4 us

profile of v4, /device:TPU:0, one launch (start us, length us, event | category | flops | bytes accessed | tf_op | source)
XLA Modules:
  0.0 60.3 jit_solution(11810506055081551114)
XLA Ops:
  0.0 59.4 %shard_map.17 = f32[256,1024]{1,0:T(8,128)S(1)} custom-call(bf16[1024,2,1024]{2,1,0:T(2,128)(2,1)} %frames_ref.1), custom_call_target="tpu_custom_call" | custom-call | flops 2147483648 | bytes 4194304 | tf_op jit(solution)/shard_map/pallas_call | solution.py:289
  59.4 1.0 %copy.3 = f32[256,1024]{1,0:T(8,128)} copy(f32[256,1024]{1,0:T(8,128)S(1)} %shard_map.17) | data formatting | bytes 2097152
